TPU v7x, 32 devices: a whole 2x2x4 slice. The times are simulated.
32 devices in a mesh: req: 8 (over y, x, core), hid: 4 (over z).
Axes of the slice: x: 2, y: 2, z: 4, core: 2. Of those that a mesh axis runs over, the one named last changes fastest.
Arguments:
- tokens: bfloat16 [16, 16, 2, 4096], P('req', 'hid'), may hold values from -6 to 6
- input_gain: float32 [4096], replicated, may hold values from 0.1 to 1.9
- qkv_weight: bfloat16 [4096, 3, 4096], P(None, None, 'hid'), may hold values from -0.09375 to 0.09375
- out_weight: bfloat16 [4096, 4096], P('hid'), may hold values from -0.375 to 0.375
- in_weight: bfloat16 [4096, 16384], P(None, ('req', 'hid')), may hold values from -0.09375 to 0.09375
- down_weight: bfloat16 [16384, 4096], P(('req', 'hid')), may hold values from -0.046875 to 0.046875
- final_gain: float32 [4096], replicated, may hold values from 0.1 to 1.9
- score_weight: bfloat16 [4096], replicated, may hold values from -0.09375 to 0.09375
- prompt_keys: bfloat16 [16, 2048, 4096], P('req', None, 'hid'), may hold values from -260 to 260
- prompt_values: bfloat16 [16, 2048, 4096], P('req', None, 'hid'), may hold values from -6 to 6
- tail_keys: bfloat16 [16, 16, 64, 4096], P('req', None, None, 'hid'), may hold values from -12 to 12
- tail_values: bfloat16 [16, 16, 64, 4096], P('req', None, None, 'hid'), may hold values from -6 to 6
- prompt_lengths: int32 [16], P('req'), may hold values from 1 to 2048
- tail_lengths: int32 [16, 16], P('req'), may hold values from 0 to 64
Outputs:
- next_hidden: bfloat16 [16, 16, 2, 4096], P('req', 'hid')
- sample_scores: float32 [16, 16, 2], P('req', 'hid')
Inputs may be any that keep to these rules, and one draw needn't show every extreme that they name: `prompt_lengths`: a request's prompt occupies positions 0 to its length - 1. `tail_lengths`: a sample's tail occupies positions 0 to its length - 1.
All inputs are finite; a program needn't handle non-finite values.
Results may differ from a plain program's by a relative error of at most 0.017.
Values may be sent and summed in bfloat16 or wider, within the bound.
A program may use at most 192 MiB of HBM per device.

v0:
```python
import jax
import jax.numpy as jnp
from jax import lax
from jax.sharding import PartitionSpec as P

HEAD_DIM = 256
ROT = 64


very_low = -1e30


def layer_norm(values, gain):
    centre = jnp.mean(values, axis=-1, keepdims=True)
    centred = values - centre
    spread = jnp.mean(centred * centred, axis=-1, keepdims=True)
    return centred * lax.rsqrt(spread + 1e-05) * gain


def rotate(vectors, positions):
    half_rot = ROT // 2
    frequency = 10000.0 ** (-(jnp.arange(half_rot, dtype=jnp.float32) * (2.0 / ROT)))
    angles = positions.astype(jnp.float32)[..., None] * frequency
    cosine = jnp.cos(angles)[..., None, :]
    sine_part = jnp.sin(angles)[..., None, :]
    paired = vectors[..., :ROT].reshape(vectors.shape[:-1] + (half_rot, 2))
    even_part = paired[..., 0]
    odd_part = paired[..., 1]
    turned = jnp.stack(
        [even_part * cosine - odd_part * sine_part, odd_part * cosine + even_part * sine_part],
        axis=-1,
    )
    return jnp.concatenate(
        [turned.reshape(vectors.shape[:-1] + (ROT,)), vectors[..., ROT:]], axis=-1
    )


def shards(
    tokens,
    input_gain,
    qkv_weight,
    out_weight,
    in_weight,
    down_weight,
    final_gain,
    score_weight,
    prompt_keys,
    prompt_values,
    tail_keys,
    tail_values,
    prompt_lengths,
    tail_lengths,
):
    req_dev, samp_dev, fresh, width = tokens.shape
    own_rows = req_dev * samp_dev * fresh
    residual = tokens.astype(jnp.float32).reshape(own_rows, width)
    normed = layer_norm(residual, input_gain).astype(jnp.bfloat16)
    gathered = lax.all_gather(normed, ("req", "hid"), axis=0, tiled=True)
    hidden_units = jax.nn.gelu(
        jnp.dot(gathered, in_weight, preferred_element_type=jnp.float32), approximate=True
    ).astype(jnp.bfloat16)
    slab_rows, triple, slab_cols = qkv_weight.shape
    flat_qkv = qkv_weight.reshape(slab_rows, triple * slab_cols)
    hid_count = lax.axis_size("hid")
    group_rows = own_rows * hid_count
    group_normed = lax.dynamic_slice_in_dim(
        gathered, lax.axis_index("req") * group_rows, group_rows, 0
    )
    mixed_qkv = jnp.dot(group_normed, flat_qkv, preferred_element_type=jnp.float32).astype(
        jnp.bfloat16
    )
    heads_here = slab_cols // HEAD_DIM
    samples = hid_count * samp_dev
    grouped = mixed_qkv.reshape(hid_count, req_dev, samp_dev, fresh, triple, heads_here, HEAD_DIM)
    grouped = jnp.transpose(grouped, (1, 0, 2, 3, 4, 5, 6)).reshape(
        req_dev, samples, fresh, triple, heads_here, HEAD_DIM
    )
    positions = (
        prompt_lengths[:, None, None]
        + tail_lengths[:, :, None]
        + jnp.arange(fresh, dtype=jnp.int32)[None, None, :]
    )
    queries = rotate(grouped[:, :, :, 0].astype(jnp.float32), positions).astype(jnp.bfloat16)
    new_keys = rotate(grouped[:, :, :, 1].astype(jnp.float32), positions).astype(jnp.bfloat16)
    new_values = grouped[:, :, :, 2]
    prompt_len = prompt_keys.shape[1]
    cached_keys = prompt_keys.reshape(req_dev, prompt_len, heads_here, HEAD_DIM)
    cached_values = prompt_values.reshape(req_dev, prompt_len, heads_here, HEAD_DIM)
    prompt_queries = queries.reshape(req_dev, samples * fresh, heads_here, HEAD_DIM)
    score_scale = HEAD_DIM ** (-0.5)
    prompt_scores = (
        jnp.einsum(
            "rqhd,rkhd->rqhk", prompt_queries, cached_keys, preferred_element_type=jnp.float32
        )
        * score_scale
    )
    keeping = (jnp.arange(prompt_len, dtype=jnp.int32)[None, :] < prompt_lengths[:, None])[
        :, None, None, :
    ]
    prompt_scores = jnp.where(keeping, prompt_scores, very_low)
    peaks = jnp.max(prompt_scores, axis=-1)
    prompt_weights = jnp.where(keeping, jnp.exp(prompt_scores - peaks[..., None]), 0.0)
    totals = jnp.sum(prompt_weights, axis=-1)
    accrued = jnp.einsum(
        "rqhk,rkhd->rqhd",
        prompt_weights.astype(jnp.bfloat16),
        cached_values,
        preferred_element_type=jnp.float32,
    )
    peaks = peaks.reshape(req_dev, samples, fresh, heads_here)
    totals = totals.reshape(req_dev, samples, fresh, heads_here)
    accrued = accrued.reshape(req_dev, samples, fresh, heads_here, HEAD_DIM)
    tail_len = tail_keys.shape[2]
    later_keys = tail_keys.reshape(req_dev, samples, tail_len, heads_here, HEAD_DIM)
    later_values = tail_values.reshape(req_dev, samples, tail_len, heads_here, HEAD_DIM)
    tail_scores = (
        jnp.einsum("rsthd,rskhd->rsthk", queries, later_keys, preferred_element_type=jnp.float32)
        * score_scale
    )
    tail_keep = (jnp.arange(tail_len, dtype=jnp.int32)[None, None, :] < tail_lengths[:, :, None])[
        :, :, None, None, :
    ]
    self_scores = (
        jnp.einsum("rsthd,rsuhd->rsthu", queries, new_keys, preferred_element_type=jnp.float32)
        * score_scale
    )
    position_order = jnp.arange(fresh, dtype=jnp.int32)
    self_keep = (position_order[None, :] <= position_order[:, None])[None, None, :, None, :]
    highest = jnp.maximum(peaks, jnp.max(jnp.where(tail_keep, tail_scores, very_low), axis=-1))
    highest = jnp.maximum(highest, jnp.max(jnp.where(self_keep, self_scores, very_low), axis=-1))
    scaling = jnp.exp(peaks - highest)
    tail_weights = jnp.where(tail_keep, jnp.exp(tail_scores - highest[..., None]), 0.0)
    self_weights = jnp.where(self_keep, jnp.exp(self_scores - highest[..., None]), 0.0)
    totals = totals * scaling + jnp.sum(tail_weights, axis=-1) + jnp.sum(self_weights, axis=-1)
    accrued = accrued * scaling[..., None]
    accrued = accrued + jnp.einsum(
        "rsthk,rskhd->rsthd",
        tail_weights.astype(jnp.bfloat16),
        later_values,
        preferred_element_type=jnp.float32,
    )
    accrued = accrued + jnp.einsum(
        "rsthu,rsuhd->rsthd",
        self_weights.astype(jnp.bfloat16),
        new_values,
        preferred_element_type=jnp.float32,
    )
    attended = (accrued / totals[..., None]).astype(jnp.bfloat16)
    attended = attended.reshape(req_dev, hid_count, samp_dev, fresh, heads_here * HEAD_DIM)
    attended_rows = jnp.transpose(attended, (1, 0, 2, 3, 4)).reshape(
        group_rows, heads_here * HEAD_DIM
    )
    mlp_part = lax.psum_scatter(
        jnp.dot(hidden_units, down_weight, preferred_element_type=jnp.float32),
        ("req", "hid"),
        scatter_dimension=0,
        tiled=True,
    )
    projection_part = lax.psum_scatter(
        jnp.dot(attended_rows, out_weight, preferred_element_type=jnp.float32).astype(jnp.bfloat16),
        "hid",
        scatter_dimension=0,
        tiled=True,
    ).astype(jnp.float32)
    branch_sum = mlp_part + projection_part
    final_state = residual + branch_sum
    next_hidden = final_state.astype(jnp.bfloat16).reshape(req_dev, samp_dev, fresh, width)
    sample_scores = jnp.sum(
        layer_norm(final_state, final_gain) * score_weight.astype(jnp.float32), axis=-1
    )
    return (next_hidden, sample_scores.reshape(req_dev, samp_dev, fresh))


def solution(mesh):
    placed = (
        P("req", "hid", None, None),
        P(),
        P(None, None, "hid"),
        P("hid", None),
        P(None, ("req", "hid")),
        P(("req", "hid"), None),
        P(),
        P(),
        P("req", None, "hid"),
        P("req", None, "hid"),
        P("req", None, None, "hid"),
        P("req", None, None, "hid"),
        P("req"),
        P("req", None),
    )
    return jax.shard_map(
        shards,
        mesh=mesh,
        in_specs=placed,
        out_specs=(P("req", "hid", None, None), P("req", "hid", None)),
        check_vma=False,
    )
```

profile of v0, /device:TPU:0, one launch (start us, length us, event | category | flops | bytes accessed | tf_op | source)
XLA Modules:
  0.0 340.8 jit_solution(5207339250362913866)
XLA Ops:
  7.2 0.9 reshape.217
  8.2 1.1 convert_reduce_fusion
  9.3 1.2 multiply_reduce_fusion.2
  10.5 0.1 div.23
  10.6 0.1 rsqrt.20
  10.7 1.5 multiply_convert_fusion
  12.3 33.5 %copy.133 = bf16[4096,3,1024]{0,2,1:T(8,128)(2,1)} copy(bf16[4096,3,1024]{2,0,1:T(8,128)(2,1)} %param.16) | data formatting | bytes 50331648 | tf_op args[2]
  45.8 0.1 broadcast_add_fusion
  45.9 0.1 iota_compare_fusion
  45.9 0.3 multiply_cosine_fusion
  46.2 0.1 iota_compare_fusion.1
  46.3 30.8 %all-gather.2.cloned.1.call-done = bf16[512,4096]{1,0:T(8,128)(2,1)} async-done(((bf16[16,4096]{1,0:T(8,128)(2,1)}), bf16[512,4096]{1,0:T(8,128)(2,1)}) %all-gather.2.cloned.1.call-update) | async-done | bytes 4194320 | tf_op jit(solution)/shard_map/all_gather | solution.py:58
  77.1 12.5 %convolution_convert_fusion.1 = bf16[64,3072]{1,0:T(8,128)(2,1)S(1)} fusion(bf16[4096,3072]{0,1:T(8,128)(2,1)} %bitcast.115, bf16[512,4096]{1,0:T(8,128)(2,1)} %all-gather.2.cloned.1.call-done, s32[]{:T(128)S(6)} %select_n.27), kind=kOutput, calls=%fused_computation.13 | convolution fusion | flops 1610809344 | bytes 26083332 | tf_op jit(solution)/shard_map/dot_general | solution.py:69
  89.6 0.3 reshape.219
  89.9 0.2 copy.226
  90.1 0.1 reshape.220
  90.3 0.1 slice.72
  90.4 0.1 slice.55
  90.5 0.2 copy.135
  90.7 0.7 multiply_subtract_fusion
  91.4 0.7 maximum_convert_fusion
  92.1 2.7 copy.136
  94.8 0.1 copy.143
  95.0 0.2 copy.148
  95.2 0.7 subtract_convert_fusion
  95.9 0.7 pad_maximum_fusion
  96.6 0.1 copy.149
  96.8 0.1 pad_maximum_fusion.1
  96.9 0.3 fusion.65
  97.2 0.2 copy.152
  97.4 3.5 %select_reduce_fusion = (f32[2,16,2,4]{2,3,1,0:T(4,128)S(1)}, f32[2,16,2,4,64]{4,2,3,1,0:T(2,128)S(1)}) fusion(pred[2,16,64]{2,1,0:T(8,128)(4,1)S(1)} %iota_compare_fusion, bf16[2,16,8,4,8,256]{5,4,3,2,1,0:T(8,128)(2,1)} %bitcast.139, bf16[2,16,2,4,256]{4,1,3,2,0:T(8,128)(2,1)S(1)} %get-tuple-element.35), kind=kOutput, calls=%fused_computation.71 | convolution fusion | flops 8437504 | bytes 4393984 | tf_op jit(solution)/shard_map/rsthd,rskhd->rsthk/dot_general | solution.py:117
  100.9 0.1 copy.147
  101.0 0.5 copy.138
  101.6 6.1 %fusion.85 = (f32[2,32,4]{1,2,0:T(4,128)S(1)}, f32[2,32,4,2048]{3,1,2,0:T(8,128)S(1)}) fusion(bf16[2,256,4,8,256]{4,3,2,1,0:T(8,128)(2,1)} %bitcast.116, bf16[2,32,4,192]{3,1,2,0:T(8,128)(2,1)S(1)} %copy.139, bf16[2,32,4,64]{3,1,2,0:T(8,128)(2,1)S(1)} %copy.138, pred[2,2048]{1,0:T(4,128)(4,1)S(1)} %iota_compare_fusion.1), kind=kOutput, calls=%fused_computation.112 | convolution fusion | flops 270270208 | bytes 10621952 | tf_op jit(solution)/shard_map/rqhd,rkhd->rqhk/dot_general | solution.py:92
  107.7 0.1 copy.142
  107.8 0.1 copy.155
  107.9 0.1 fusion.70
  108.0 0.1 copy.158
  108.1 0.1 fusion.74
  108.2 0.5 fusion.75
  108.7 0.1 copy.164
  108.8 0.5 fusion.21
  109.3 0.1 copy.162
  109.4 0.1 copy.163
  109.5 0.1 copy.156
  109.7 5.0 %fusion.31 = f32[2,32,4,256]{3,1,2,0:T(8,128)S(1)} fusion(bf16[2,256,4,8,256]{4,3,2,1,0:T(8,128)(2,1)} %bitcast.138, f32[2,32,4,2048]{3,1,2,0:T(8,128)S(1)} %get-tuple-element.32, f32[2,32,4]{1,2,0:T(4,128)S(1)} %get-tuple-element.31, pred[2,2048]{1,0:T(4,128)(4,1)S(1)} %iota_compare_fusion.1), kind=kOutput, calls=%fused_computation.26 | convolution fusion | flops 270008320 | bytes 10753024 | tf_op jit(solution)/shard_map/rqhk,rkhd->rqhd/dot_general | solution.py:104
  114.7 0.2 reshape.224
  114.8 0.1 copy.167
  115.0 0.2 copy.161
  115.1 3.0 fusion.28
  118.1 0.3 fusion.34
  118.4 0.1 copy.168
  118.6 5.8 %convolution_convert_fusion = bf16[64,4096]{1,0:T(8,128)(2,1)} fusion(bf16[64,1024]{1,0:T(8,128)(2,1)S(1)} %reshape.234, bf16[1024,4096]{1,0:T(8,128)(2,1)} %param.17), kind=kOutput, calls=%fused_computation.6 | convolution fusion | flops 537133056 | bytes 9043968 | tf_op jit(solution)/shard_map/dot_general | solution.py:160
  124.4 0.3 reduce-scatter.3.cloned.1.call-start
  124.7 12.6 %fusion.53 = f32[512,4096]{1,0:T(8,128)} fusion(bf16[512,4096]{1,0:T(8,128)(2,1)} %param.19, bf16[512,4096]{1,0:T(8,128)(2,1)} %all-gather.2.cloned.1.call-done, bf16[4096,512]{1,0:T(8,128)(2,1)} %param.18), kind=kOutput, calls=%fused_computation.41 | convolution fusion | flops 4297326592 | bytes 20971520 | tf_op jit(solution)/shard_map/dot_general | solution.py:154
  137.3 0.7 copy-done.1
  138.0 6.7 %reduce-scatter.5.cloned.1.call-done = bf16[16,4096]{1,0:T(8,128)(2,1)} async-done(((bf16[64,4096]{1,0:T(8,128)(2,1)}), bf16[16,4096]{1,0:T(8,128)(2,1)}) %reduce-scatter.5.cloned.1.call-update) | async-done | bytes 131088 | tf_op jit(solution)/shard_map/reduce_scatter | solution.py:159
  144.7 186.4 %reduce-scatter.3.cloned.1.call-done = f32[16,4096]{1,0:T(8,128)} async-done(((f32[512,4096]{1,0:T(8,128)}), f32[16,4096]{1,0:T(8,128)}) %reduce-scatter.3.cloned.1.call-update) | async-done | bytes 262160 | tf_op jit(solution)/shard_map/reduce_scatter | solution.py:153
  331.1 1.1 fusion.84
  332.3 0.2 multiply_reduce_fusion.1
  332.5 0.2 multiply_reduce_fusion
  332.8 0.8 reshape.235
  333.5 0.1 reshape.236
  333.6 0.7 copy.169
  (28 shorter events, 0.4 us)
Async XLA Ops:
  7.2 70.0 %all-gather.2.cloned.1.call-start = ((), (), s32[]{:S(2)}) async-start(), calls=%async_computation.2 | async-start | bytes 4325376 | tf_op jit(solution)/shard_map/all_gather | solution.py:58
  12.2 132.6 %reduce-scatter.5.cloned.1.call-start = ((), (), s32[]{:S(2)}) async-start(), calls=%async_computation.4 | async-start | bytes 655360 | tf_op jit(solution)/shard_map/reduce_scatter | solution.py:159
  12.2 33.5 %copy-start.2 = (s32[2,16]{1,0:T(2,128)S(1)}, s32[2,16]{1,0:T(2,128)}, u32[]{:S(2)}) copy-start(s32[2,16]{1,0:T(2,128)} %param.27) | copy-start | bytes 388
  12.2 33.5 %copy-start.3 = (s32[2]{0:T(128)S(1)}, s32[2]{0:T(128)}, u32[]{:S(2)}) copy-start(s32[2]{0:T(128)} %param.26) | copy-start | bytes 28
  124.4 206.7 %reduce-scatter.3.cloned.1.call-start = ((), (), s32[]{:S(2)}) async-start(), calls=%async_computation.3 | async-start | bytes 8650752 | tf_op jit(solution)/shard_map/reduce_scatter | solution.py:153
  137.3 0.7 copy-start.1
  137.3 195.2 %copy-start = (f32[4096]{0:T(1024)S(1)}, f32[4096]{0:T(1024)}, u32[]{:S(2)}) copy-start(f32[4096]{0:T(1024)} %param.20) | copy-start | bytes 49156
Sparse Core Ops, SparseCore 0:
  12.3 64.7 all-gather.1
  124.5 20.1 reduce-scatter.4
  147.0 184.0 reduce-scatter.2
where the time goes:
time: 342 us; the launch traced here: 341 us
  waiting for transfers between devices  224 us (65%)
  matrix products  49 us (14%)
  local copies, waits for them, and re-layouts  43.3 us (13%)
  between operations  14 us (4%)
  other arithmetic  10.1 us (3%)
    reduce_scatter x1, waiting for transfers between devices, shards(): lax.psum_scatter(jnp.dot(hidden_units, down_weight, preferred_element_typ...  186 us
    unnamed x10, local copies, waits for them, and re-layouts  34.8 us
    all_gather x1, waiting for transfers between devices, shards(): gathered = lax.all_gather(normed, ('req', 'hid'), axis=0, tiled=True)  30.8 us
    dot_general x1, matrix products, shards(): jnp.dot(hidden_units, down_weight, preferred_element_type=jnp.float32)  12.6 us
    dot_general x1, matrix products, shards(): jnp.dot(group_normed, flat_qkv, preferred_element_type=jnp.float32)  12.5 us
  transfers between devices with their start and end apart: 3, of which 3 were waited for; matrix products, arithmetic and copies ran while one was open for 14% of the time, Pallas kernels for 0%

commit v1 on v0

--- a/solution.py
+++ b/solution.py
@@ -1,6 +1,10 @@
+import functools
+
 import jax
 import jax.numpy as jnp
 from jax import lax
+from jax.experimental import pallas as pl
+from jax.experimental.pallas import tpu as pltpu
 from jax.sharding import PartitionSpec as P
 
 HEAD_DIM = 256
@@ -33,6 +37,254 @@
     return jnp.concatenate(
         [turned.reshape(vectors.shape[:-1] + (ROT,)), vectors[..., ROT:]], axis=-1
     )
+
+
+CHUNKS = 4
+MESH = pl.DeviceIdType.MESH
+
+
+def flip(index, bit):
+    return index + bit * (1 - 2 * lax.rem(lax.div(index, bit), 2))
+
+
+def place(slot, count):
+    return slot // 2 + (slot % 2) * (count // 2)
+
+
+def greet(bits, hid_count):
+    req, hid = lax.axis_index("req"), lax.axis_index("hid")
+    barrier = pltpu.get_barrier_semaphore()
+    for bit in bits:
+        pl.semaphore_signal(barrier, inc=1, device_id=(flip(req, bit), hid), device_id_type=MESH)
+    for step in range(1, hid_count):
+        other = lax.rem(hid + step, hid_count)
+        pl.semaphore_signal(barrier, inc=1, device_id=(req, other), device_id_type=MESH)
+    return lambda: pl.semaphore_wait(barrier, len(bits) + hid_count - 1)
+
+
+def reduce_orders(req_count):
+    bits = [1 << i for i in range(req_count.bit_length() - 1)]
+    return [bits if c % 2 == 0 else bits[:1] + bits[:0:-1] for c in range(CHUNKS)]
+
+
+def gather_kernel(
+    req_count, hid_count, tok_ref, gain_ref, w_hbm, group_ref, hidden_ref,
+    full, w_ref, total, hid_send, hid_recv, req_send, req_recv, w_sem,
+):
+    req, hid = lax.axis_index("req"), lax.axis_index("hid")
+    orders = [order[::-1] for order in reduce_orders(req_count)]
+    width = tok_ref.shape[1] // CHUNKS
+    half = req_count // 2
+    greeted = greet(orders[0], hid_count)
+    w_copy = pltpu.make_async_copy(w_hbm, w_ref, w_sem)
+    w_copy.start()
+    values = tok_ref[...].astype(jnp.float32)
+    full[0, hid] = layer_norm(values, gain_ref[...]).astype(full.dtype)
+    greeted()
+    columns = [pl.ds(c * width, width) for c in range(CHUNKS)]
+    sent = []
+    arriving = [[] for _ in range(CHUNKS)]
+    for c in range(CHUNKS):
+        for step in range(1, hid_count):
+            block = full.at[0, hid, :, columns[c]]
+            copy = pltpu.make_async_remote_copy(
+                src_ref=block, dst_ref=block,
+                send_sem=hid_send.at[c, step - 1], recv_sem=hid_recv.at[c, step - 1],
+                device_id=(req, lax.rem(hid + step, hid_count)), device_id_type=MESH,
+            )
+            copy.start()
+            sent.append(copy)
+            arriving[c].append(copy)
+    held = [[0] for _ in range(CHUNKS)]
+    for stage in range(len(orders[0])):
+        for c in range(CHUNKS):
+            bit = orders[c][stage]
+            for copy in arriving[c]:
+                copy.wait_recv()
+            arriving[c] = []
+            for slot in list(held[c]):
+                there = slot ^ bit
+                copy = pltpu.make_async_remote_copy(
+                    src_ref=full.at[place(slot, req_count), :, :, columns[c]],
+                    dst_ref=full.at[place(there, req_count), :, :, columns[c]],
+                    send_sem=req_send.at[c, there - 1], recv_sem=req_recv.at[c, there - 1],
+                    device_id=(flip(req, bit), hid), device_id_type=MESH,
+                )
+                copy.start()
+                sent.append(copy)
+                arriving[c].append(copy)
+                held[c].append(there)
+        if stage == 0:
+            group_ref[...] = full[0]
+    w_copy.wait()
+    rows = half * full.shape[1] * full.shape[2]
+    for side in range(2):
+        for c in range(CHUNKS):
+            if side == 1:
+                for copy in arriving[c]:
+                    copy.wait_recv()
+            block = full[side * half : (side + 1) * half, :, :, c * width : (c + 1) * width]
+            part = jnp.dot(
+                block.reshape(rows, width), w_ref[c * width : (c + 1) * width, :],
+                preferred_element_type=jnp.float32,
+            )
+            total[...] = part if c == 0 else total[...] + part
+        hidden_ref[side] = jax.nn.gelu(total[...], approximate=True).astype(hidden_ref.dtype)
+    for copy in sent:
+        copy.wait_send()
+
+
+def reduce_kernel(
+    req_count, hid_count, hidden_ref, proj_ref, w_hbm, out_ref,
+    w_ref, part, landed, total, leaving, hid_landed,
+    w_sem, req_send, req_recv, hid_send, hid_recv,
+):
+    req, hid = lax.axis_index("req"), lax.axis_index("hid")
+    orders = reduce_orders(req_count)
+    half = req_count // 2
+    width = part.shape[-1]
+    block_shape = (half,) + part.shape[2:]
+    greeted = greet(orders[0], hid_count)
+    w_copies = []
+    for c in range(CHUNKS):
+        copy = pltpu.make_async_copy(
+            w_hbm.at[:, pl.ds(c * width, width)], w_ref.at[c], w_sem.at[c]
+        )
+        copy.start()
+        w_copies.append(copy)
+    sent = []
+
+    def send(c, slot, bit):
+        copy = pltpu.make_async_remote_copy(
+            src_ref=part.at[c, place(slot, req_count)], dst_ref=landed.at[c, slot - 1],
+            send_sem=req_send.at[c, slot - 1], recv_sem=req_recv.at[c, slot - 1],
+            device_id=(flip(req, bit), hid), device_id_type=MESH,
+        )
+        copy.start()
+        sent.append(copy)
+        return copy
+
+    active = [list(range(req_count)) for _ in range(CHUNKS)]
+    arriving = [{} for _ in range(CHUNKS)]
+    for c in range(CHUNKS):
+        w_copies[c].wait()
+        for side in (1, 0):
+            value = jnp.dot(hidden_ref[side], w_ref[c], preferred_element_type=jnp.float32)
+            part[c, side * half : (side + 1) * half] = value.astype(part.dtype).reshape(block_shape)
+            if side == 1:
+                if c == 0:
+                    greeted()
+                for slot in range(1, req_count, 2):
+                    arriving[c][slot] = send(c, slot, 1)
+        active[c] = list(range(0, req_count, 2))
+    for stage in range(1, len(orders[0])):
+        for c in range(CHUNKS):
+            before, bit = orders[c][stage - 1], orders[c][stage]
+            landing, arriving[c] = arriving[c], {}
+            for slot in sorted(active[c], key=lambda s: -(s & bit)):
+                landing[slot | before].wait_recv()
+                at = place(slot, req_count)
+                both = part[c, at].astype(jnp.float32) + landed[c, (slot | before) - 1].astype(
+                    jnp.float32
+                )
+                part[c, at] = both.astype(part.dtype)
+                if slot & bit:
+                    arriving[c][slot] = send(c, slot, bit)
+            active[c] = [slot for slot in active[c] if not slot & bit]
+    hid_copies = []
+    for c in range(CHUNKS):
+        last = orders[c][-1]
+        arriving[c][last].wait_recv()
+        both = part[c, 0].astype(jnp.float32) + landed[c, last - 1].astype(jnp.float32)
+        both = both + proj_ref[:, :, c * width : (c + 1) * width]
+        total[c] = both
+        leaving[c] = both.astype(leaving.dtype)
+        for step in range(1, hid_count):
+            other = lax.rem(hid + step, hid_count)
+            copy = pltpu.make_async_remote_copy(
+                src_ref=leaving.at[c, other], dst_ref=hid_landed.at[c, step - 1],
+                send_sem=hid_send.at[c, step - 1], recv_sem=hid_recv.at[c, step - 1],
+                device_id=(req, other), device_id_type=MESH,
+            )
+            copy.start()
+            sent.append(copy)
+            hid_copies.append(copy)
+    for c in range(CHUNKS):
+        value = total[c, hid]
+        for step in range(1, hid_count):
+            hid_copies[c * (hid_count - 1) + step - 1].wait_recv()
+            value = value + hid_landed[c, step - 1].astype(jnp.float32)
+        out_ref[:, c * width : (c + 1) * width] = value
+    for copy in sent:
+        copy.wait_send()
+
+
+def in_vmem(count):
+    return [pl.BlockSpec(memory_space=pltpu.VMEM)] * count
+
+
+def params(collective_id):
+    return pltpu.CompilerParams(
+        collective_id=collective_id, has_side_effects=True, vmem_limit_bytes=48 * 2**20
+    )
+
+
+def gather_up(own_tokens, gain, in_weight):
+    req_count, hid_count = lax.axis_size("req"), lax.axis_size("hid")
+    rows, width = own_tokens.shape
+    units = in_weight.shape[1]
+    side_rows = req_count // 2 * hid_count * rows
+    dma = pltpu.SemaphoreType.DMA
+    return pl.pallas_call(
+        functools.partial(gather_kernel, req_count, hid_count),
+        out_shape=(
+            jax.ShapeDtypeStruct((hid_count, rows, width), jnp.bfloat16),
+            jax.ShapeDtypeStruct((2, side_rows, units), jnp.bfloat16),
+        ),
+        in_specs=in_vmem(2) + [pl.BlockSpec(memory_space=pl.ANY)],
+        out_specs=tuple(in_vmem(2)),
+        scratch_shapes=[
+            pltpu.VMEM((req_count, hid_count, rows, width), jnp.bfloat16),
+            pltpu.VMEM((width, units), jnp.bfloat16),
+            pltpu.VMEM((side_rows, units), jnp.float32),
+            dma((CHUNKS, hid_count - 1)),
+            dma((CHUNKS, hid_count - 1)),
+            dma((CHUNKS, req_count - 1)),
+            dma((CHUNKS, req_count - 1)),
+            dma(()),
+        ],
+        compiler_params=params(0),
+        name="gather_up",
+    )(own_tokens, gain.reshape(1, width), in_weight)
+
+
+def down_reduce(hidden_units, projected, down_weight):
+    req_count, hid_count = lax.axis_size("req"), lax.axis_size("hid")
+    _, rows, width = projected.shape
+    units = down_weight.shape[0]
+    part_width = width // CHUNKS
+    dma = pltpu.SemaphoreType.DMA
+    return pl.pallas_call(
+        functools.partial(reduce_kernel, req_count, hid_count),
+        out_shape=jax.ShapeDtypeStruct((rows, width), jnp.float32),
+        in_specs=in_vmem(2) + [pl.BlockSpec(memory_space=pl.ANY)],
+        out_specs=in_vmem(1)[0],
+        scratch_shapes=[
+            pltpu.VMEM((CHUNKS, units, part_width), jnp.bfloat16),
+            pltpu.VMEM((CHUNKS, req_count, hid_count, rows, part_width), jnp.bfloat16),
+            pltpu.VMEM((CHUNKS, req_count - 1, hid_count, rows, part_width), jnp.bfloat16),
+            pltpu.VMEM((CHUNKS, hid_count, rows, part_width), jnp.float32),
+            pltpu.VMEM((CHUNKS, hid_count, rows, part_width), jnp.bfloat16),
+            pltpu.VMEM((CHUNKS, hid_count - 1, rows, part_width), jnp.bfloat16),
+            dma((CHUNKS,)),
+            dma((CHUNKS, req_count - 1)),
+            dma((CHUNKS, req_count - 1)),
+            dma((CHUNKS, hid_count - 1)),
+            dma((CHUNKS, hid_count - 1)),
+        ],
+        compiler_params=params(1),
+        name="down_reduce",
+    )(hidden_units, projected, down_weight)
 
 
 def shards(
@@ -53,22 +305,19 @@
 ):
     req_dev, samp_dev, fresh, width = tokens.shape
     own_rows = req_dev * samp_dev * fresh
-    residual = tokens.astype(jnp.float32).reshape(own_rows, width)
-    normed = layer_norm(residual, input_gain).astype(jnp.bfloat16)
-    gathered = lax.all_gather(normed, ("req", "hid"), axis=0, tiled=True)
-    hidden_units = jax.nn.gelu(
-        jnp.dot(gathered, in_weight, preferred_element_type=jnp.float32), approximate=True
-    ).astype(jnp.bfloat16)
+    own_tokens = tokens.reshape(own_rows, width)
+    residual = own_tokens.astype(jnp.float32)
+    group_normed, hidden_units = gather_up(own_tokens, input_gain, in_weight)
     slab_rows, triple, slab_cols = qkv_weight.shape
-    flat_qkv = qkv_weight.reshape(slab_rows, triple * slab_cols)
     hid_count = lax.axis_size("hid")
     group_rows = own_rows * hid_count
-    group_normed = lax.dynamic_slice_in_dim(
-        gathered, lax.axis_index("req") * group_rows, group_rows, 0
-    )
-    mixed_qkv = jnp.dot(group_normed, flat_qkv, preferred_element_type=jnp.float32).astype(
-        jnp.bfloat16
-    )
+    mixed_qkv = jnp.einsum(
+        "nd,jdc->jnc",
+        group_normed.reshape(group_rows, width),
+        jnp.transpose(qkv_weight, (1, 0, 2)),
+        preferred_element_type=jnp.float32,
+    ).astype(jnp.bfloat16)
+    mixed_qkv = jnp.transpose(mixed_qkv, (1, 0, 2))
     heads_here = slab_cols // HEAD_DIM
     samples = hid_count * samp_dev
     grouped = mixed_qkv.reshape(hid_count, req_dev, samp_dev, fresh, triple, heads_here, HEAD_DIM)
@@ -150,19 +399,10 @@
     attended_rows = jnp.transpose(attended, (1, 0, 2, 3, 4)).reshape(
         group_rows, heads_here * HEAD_DIM
     )
-    mlp_part = lax.psum_scatter(
-        jnp.dot(hidden_units, down_weight, preferred_element_type=jnp.float32),
-        ("req", "hid"),
-        scatter_dimension=0,
-        tiled=True,
-    )
-    projection_part = lax.psum_scatter(
-        jnp.dot(attended_rows, out_weight, preferred_element_type=jnp.float32).astype(jnp.bfloat16),
-        "hid",
-        scatter_dimension=0,
-        tiled=True,
-    ).astype(jnp.float32)
-    branch_sum = mlp_part + projection_part
+    projected = jnp.dot(attended_rows, out_weight, preferred_element_type=jnp.float32)
+    branch_sum = down_reduce(
+        hidden_units, projected.reshape(hid_count, own_rows, width), down_weight
+    )
     final_state = residual + branch_sum
     next_hidden = final_state.astype(jnp.bfloat16).reshape(req_dev, samp_dev, fresh, width)
     sample_scores = jnp.sum(

time: 342 us -> 127 us (0.37)
  waiting for transfers between devices: 224 us -> 0 us
  Pallas kernels: 0 us -> 72.4 us
  local copies, waits for them, and re-layouts: 43.3 us -> 11.8 us
  matrix products: 49 us -> 33.8 us
  between operations: 14 us -> 0.93 us
    reduce_scatter x2 -> x0, waiting for transfers between devices: 193 us -> none  [the longest x1 186 us: shards(): lax.psum_scatter(jnp.dot(hidden_units, down_weight, preferred_element_typ...]
    pallas_call x0 -> x2, Pallas kernels: none -> 72.4 us  [the longest x1 36.3 us: gather_up(): pl.pallas_call(functools.partial(gather_kernel, req_count, hid_count), ou...]
    unnamed x10 -> x9, local copies, waits for them, and re-layouts: 34.8 us -> 3.59 us
    all_gather x1 -> x0, waiting for transfers between devices: 30.8 us -> none  [shards(): gathered = lax.all_gather(normed, ('req', 'hid'), axis=0, tiled=True)]
    dot_general x2 -> x1, matrix products: 25.1 us -> 10.5 us  [shards(): jnp.einsum('nd,jdc->jnc', group_normed.reshape(group_rows, width), jnp.tr...]
  transfers between devices with their start and end apart: 3 -> 0, of which waited for: 3 -> 0; matrix products, arithmetic and copies ran while one was open for 14% -> 0% of each run, Pallas kernels for 0% -> 0%
where the time goes in v1:
time: 127 us
  Pallas kernels  72.4 us (57%)
  matrix products  33.8 us (27%)
  local copies, waits for them, and re-layouts  11.8 us (9%)
  other arithmetic  8.06 us (6%)
    pallas_call x1, Pallas kernels, gather_up(): pl.pallas_call(functools.partial(gather_kernel, req_count, hid_count), ou...  36.3 us
    pallas_call x1, Pallas kernels, down_reduce(): pl.pallas_call(functools.partial(reduce_kernel, req_count, hid_count), ou...  36.1 us
    dot_general x1, matrix products, shards(): jnp.einsum('nd,jdc->jnc', group_normed.reshape(group_rows, width), jnp.tr...  10.5 us
    dot_general x1, matrix products, shards(): jnp.einsum('rqhd,rkhd->rqhk', prompt_queries, cached_keys, preferred_elem...  6.08 us
    dot_general x1, matrix products, shards(): jnp.dot(attended_rows, out_weight, preferred_element_type=jnp.float32)  5.12 us
    dot_general x1, matrix products, shards(): jnp.einsum('rqhk,rkhd->rqhd', prompt_weights.astype(jnp.bfloat16), cached...  5.05 us
    unnamed x9, local copies, waits for them, and re-layouts  3.59 us
    dot_general x1, matrix products, shards(): jnp.einsum('rsthd,rskhd->rsthk', queries, later_keys, preferred_element_t...  3.48 us

profile of v1, /device:TPU:0, one launch (start us, length us, event | category | flops | bytes accessed | tf_op | source)
XLA Modules:
  0.0 127.0 jit_solution(9610816958173241981)
XLA Ops:
  0.7 0.8 broadcast_add_fusion
  1.4 0.8 iota_compare_fusion
  2.2 0.7 iota_compare_fusion.1
  2.9 0.7 convert_element_type.57
  3.6 0.3 multiply_cosine_fusion
  3.9 1.0 reshape.188.tok_ref
  4.9 0.0 copy-start
  4.9 2.2 %copy-done = bf16[4096,512]{1,0:T(8,128)(2,1)S(1)} copy-done((bf16[4096,512]{1,0:T(8,128)(2,1)S(1)}, bf16[4096,512]{1,0:T(8,128)(2,1)}, u32[]{:S(2)}) %copy-start) | copy-done | bytes 4194328
  7.1 0.0 copy-start.2
  7.1 0.7 copy-done.2
  7.8 36.3 %gather_up.1 = (bf16[4,16,4096]{2,1,0:T(8,128)(2,1)S(1)}, bf16[2,256,512]{2,1,0:T(8,128)(2,1)S(1)}) custom-call(bf16[16,4096]{1,0:T(8,128)(2,1)S(1)} %reshape.188.tok_ref, f32[1,4096]{1,0:T(1,128)S(1)} %bitcast.125, bf16[4096,512]{1,0:T(8,128)(2,1)S(1)} %copy-done), custom_call_target="tpu_custom_call" | custom-call | tf_op jit(solution)/shard_map/gather_up/pallas_call | solution.py:238
  44.1 10.5 %fusion.27 = bf16[64,3,1024]{2,0,1:T(8,128)(2,1)S(1)} fusion(bf16[64,4096,1]{1,0,2:T(8,128)(2,1)S(1)} %bitcast.124, bf16[4096,3,1024]{2,0,1:T(8,128)(2,1)} %param.16), kind=kOutput, calls=%fused_computation.22 | convolution fusion | flops 1610809344 | bytes 26083328 | tf_op jit(solution)/shard_map/nd,jdc->jnc/dot_general | solution.py:314
  54.6 0.3 reshape.191
  54.9 0.2 copy.227
  55.1 0.1 reshape.192
  55.2 0.1 slice.72
  55.3 0.1 copy.135
  55.4 0.1 slice.55
  55.6 0.2 copy.146
  55.8 0.7 subtract_convert_fusion
  56.5 0.7 pad_maximum_fusion
  57.2 0.1 copy.147
  57.3 0.2 copy.133
  57.5 0.7 multiply_subtract_fusion
  58.2 0.7 maximum_convert_fusion
  58.9 0.1 copy.141
  59.0 0.2 pad_maximum_fusion.1
  59.2 0.3 fusion.58
  59.5 0.2 copy.150
  59.7 0.1 fusion.65
  59.8 3.5 %select_reduce_fusion = (f32[2,16,2,4]{2,3,1,0:T(4,128)S(1)}, f32[2,16,2,4,64]{4,2,3,1,0:T(2,128)S(1)}) fusion(pred[2,16,64]{2,1,0:T(8,128)(4,1)S(1)} %iota_compare_fusion, bf16[2,16,8,4,8,256]{5,4,3,2,1,0:T(8,128)(2,1)} %bitcast.150, bf16[2,16,2,4,256]{4,1,3,2,0:T(8,128)(2,1)S(1)} %get-tuple-element.37), kind=kOutput, calls=%fused_computation.58 | convolution fusion | flops 8437504 | bytes 4393984 | tf_op jit(solution)/shard_map/rsthd,rskhd->rsthk/dot_general | solution.py:366
  63.3 0.1 copy.145
  63.4 2.7 %copy.134 = bf16[2,16,2,4,32,2]{3,5,4,2,1,0:T(2,128)(2,1)S(1)} copy(bf16[2,16,2,4,32,2]{1,5,4,3,2,0:T(2,128)(2,1)S(1)} %maximum_convert_fusion) | data formatting | bytes 65536 | tf_op jit(solution)/shard_map/convert.14
  66.1 0.5 copy.136
  66.6 6.1 %fusion.74 = (f32[2,32,4]{1,2,0:T(4,128)S(1)}, f32[2,32,4,2048]{3,1,2,0:T(8,128)S(1)}) fusion(bf16[2,256,4,8,256]{4,3,2,1,0:T(8,128)(2,1)} %bitcast.126, bf16[2,32,4,192]{3,1,2,0:T(8,128)(2,1)S(1)} %copy.137, bf16[2,32,4,64]{3,1,2,0:T(8,128)(2,1)S(1)} %copy.136, pred[2,2048]{1,0:T(4,128)(4,1)S(1)} %iota_compare_fusion.1), kind=kOutput, calls=%fused_computation.92 | convolution fusion | flops 270270208 | bytes 10621952 | tf_op jit(solution)/shard_map/rqhd,rkhd->rqhk/dot_general | solution.py:341
  72.7 0.5 fusion.25
  73.3 5.1 %fusion.38 = f32[2,32,4,256]{3,1,2,0:T(8,128)S(1)} fusion(bf16[2,256,4,8,256]{4,3,2,1,0:T(8,128)(2,1)} %bitcast.149, f32[2,32,4,2048]{3,1,2,0:T(8,128)S(1)} %get-tuple-element.34, f32[2,32,4]{1,2,0:T(4,128)S(1)} %get-tuple-element.33, pred[2,2048]{1,0:T(4,128)(4,1)S(1)} %iota_compare_fusion.1), kind=kOutput, calls=%fused_computation.28 | convolution fusion | flops 270008320 | bytes 10753024 | tf_op jit(solution)/shard_map/rqhk,rkhd->rqhd/dot_general | solution.py:353
  78.3 0.2 reshape.196
  78.5 0.1 copy.140
  78.6 0.1 copy.153
  78.7 0.1 fusion.69
  78.8 0.1 copy.160
  78.9 0.1 copy.161
  79.0 0.2 copy.159
  79.1 0.1 copy.156
  79.3 0.5 fusion.70
  79.7 0.1 copy.162
  79.9 0.1 copy.165
  80.0 0.1 copy.154
  80.1 3.0 %fusion.35 = f32[2,16,2,4,256]{4,2,3,1,0:T(2,128)S(1)} fusion(bf16[2,16,8,4,8,256]{5,4,3,2,1,0:T(8,128)(2,1)} %bitcast.151, f32[2,16,2,4,256]{4,2,1,3,0:T(2,128)S(1)} %reshape.196, f32[2,16,2,4]{2,3,1,0:T(4,128)S(1)} %copy.154, f32[2,16,2,4,64]{4,2,3,1,0:T(2,128)S(1)} %get-tuple-element.36, pred[2,16,64]{2,1,0:T(8,128)(4,1)S(1)} %iota_compare_fusion, ...), kind=kOutput, calls=%fused_computation.27 | convolution fusion | flops 8568832 | bytes 4788224 | tf_op jit(solution)/shard_map/rsthk,rskhd->rsthd/dot_general | solution.py:385
  83.1 0.3 fusion.41
  83.4 0.1 copy.166
  83.5 0.0 copy-start.1
  83.5 5.1 %fusion.8.proj_ref = f32[4,16,4096]{2,1,0:T(8,128)S(1)} fusion(bf16[1024,4096]{1,0:T(8,128)(2,1)} %param.17, bf16[4,16,1024]{2,0,1:T(4,128)(2,1)S(1)} %bitcast.133), kind=kOutput, calls=%fused_computation.8 | convolution fusion | flops 536870912 | bytes 9568256 | tf_op jit(solution)/shard_map/dot_general | solution.py:402
  88.7 0.0 copy-done.1
  88.7 0.0 copy-start.3
  88.7 36.1 %down_reduce.1 = f32[16,4096]{1,0:T(8,128)S(1)} custom-call(bf16[2,256,512]{2,1,0:T(8,128)(2,1)S(1)} %get-tuple-element.4.hidden_ref, f32[4,16,4096]{2,1,0:T(8,128)S(1)} %fusion.8.proj_ref, bf16[512,4096]{1,0:T(8,128)(2,1)S(1)} %copy-done.1), custom_call_target="tpu_custom_call" | custom-call | tf_op jit(solution)/shard_map/down_reduce/pallas_call | solution.py:267
  124.8 0.2 fusion.63
  125.0 0.2 multiply_reduce_fusion.1
  125.2 0.0 copy-done.3
  125.2 0.2 multiply_reduce_fusion
  125.5 0.1 reshape.207
  125.5 0.7 copy.168
  126.2 0.8 reshape.206
  (11 shorter events, 0.1 us)
Async XLA Ops:
  4.9 2.2 %copy-start = (bf16[4096,512]{1,0:T(8,128)(2,1)S(1)}, bf16[4096,512]{1,0:T(8,128)(2,1)}, u32[]{:S(2)}) copy-start(bf16[4096,512]{1,0:T(8,128)(2,1)} %w_hbm.2) | copy-start | bytes 12582916
  7.1 0.7 copy-start.2
  83.5 5.1 %copy-start.1 = (bf16[512,4096]{1,0:T(8,128)(2,1)S(1)}, bf16[512,4096]{1,0:T(8,128)(2,1)}, u32[]{:S(2)}) copy-start(bf16[512,4096]{1,0:T(8,128)(2,1)} %w_hbm.3) | copy-start | bytes 12582916
  88.7 36.5 %copy-start.3 = (f32[4096]{0:T(1024)S(1)}, f32[4096]{0:T(1024)}, u32[]{:S(2)}) copy-start(f32[4096]{0:T(1024)} %param.20) | copy-start | bytes 49156

commit v2 on v1

--- a/solution.py
+++ b/solution.py
@@ -21,22 +21,20 @@
     return centred * lax.rsqrt(spread + 1e-05) * gain
 
 
-def rotate(vectors, positions):
-    half_rot = ROT // 2
-    frequency = 10000.0 ** (-(jnp.arange(half_rot, dtype=jnp.float32) * (2.0 / ROT)))
-    angles = positions.astype(jnp.float32)[..., None] * frequency
-    cosine = jnp.cos(angles)[..., None, :]
-    sine_part = jnp.sin(angles)[..., None, :]
-    paired = vectors[..., :ROT].reshape(vectors.shape[:-1] + (half_rot, 2))
-    even_part = paired[..., 0]
-    odd_part = paired[..., 1]
-    turned = jnp.stack(
-        [even_part * cosine - odd_part * sine_part, odd_part * cosine + even_part * sine_part],
-        axis=-1,
-    )
-    return jnp.concatenate(
-        [turned.reshape(vectors.shape[:-1] + (ROT,)), vectors[..., ROT:]], axis=-1
-    )
+def turn(vectors, table):
+    lanes = table.shape[-1]
+    first = vectors[:, :lanes]
+    even = lax.rem(lax.broadcasted_iota(jnp.int32, first.shape, 1), 2) == 0
+    other = jnp.where(even, pltpu.roll(first, lanes - 1, 1), pltpu.roll(first, 1, 1))
+    return jnp.concatenate([first * table[0] + other * table[1], vectors[:, lanes:]], axis=1)
+
+
+def rotation_table(positions):
+    lane = jnp.arange(2 * ROT, dtype=jnp.int32)
+    frequency = 10000.0 ** (-((lane // 2).astype(jnp.float32) * (2.0 / ROT)))
+    angles = positions.astype(jnp.float32)[:, None] * jnp.where(lane < ROT, frequency, 0.0)
+    sign = jnp.where(lane % 2 == 0, -1.0, 1.0)
+    return jnp.stack([jnp.cos(angles), jnp.sin(angles) * sign])
 
 
 CHUNKS = 4
@@ -68,16 +66,40 @@
 
 
 def gather_kernel(
-    req_count, hid_count, tok_ref, gain_ref, w_hbm, group_ref, hidden_ref,
-    full, w_ref, total, hid_send, hid_recv, req_send, req_recv, w_sem,
+    req_count, hid_count, tok_ref, gain_ref, table_ref, w_hbm, qkv_hbm, qkv_ref, hidden_ref,
+    full, w_ref, qkv_w, total, hid_send, hid_recv, req_send, req_recv, w_sem, qkv_sem,
 ):
     req, hid = lax.axis_index("req"), lax.axis_index("hid")
     orders = [order[::-1] for order in reduce_orders(req_count)]
     width = tok_ref.shape[1] // CHUNKS
     half = req_count // 2
     greeted = greet(orders[0], hid_count)
+    qkv_copies = []
+    for j in range(3):
+        copy = pltpu.make_async_copy(qkv_hbm.at[j], qkv_w.at[j], qkv_sem.at[j])
+        copy.start()
+        qkv_copies.append(copy)
     w_copy = pltpu.make_async_copy(w_hbm, w_ref, w_sem)
     w_copy.start()
+    _, requests, heads, request_rows, _ = qkv_ref.shape
+    own = request_rows // hid_count
+    pieces = [(j, head) for j in range(3) for head in range(heads)]
+
+    def project_one():
+        j, head = pieces.pop(0)
+        if head == 0:
+            qkv_copies[j].wait()
+        group = full[0].reshape(hid_count * full.shape[2], full.shape[3])
+        value = jnp.dot(
+            group, qkv_w[j, :, head * HEAD_DIM : (head + 1) * HEAD_DIM],
+            preferred_element_type=jnp.float32,
+        ).astype(jnp.bfloat16).astype(jnp.float32)
+        if j < 2:
+            value = turn(value, table_ref[...])
+        for r in range(requests):
+            rows = [value[(h * requests + r) * own : (h * requests + r + 1) * own] for h in range(hid_count)]
+            qkv_ref[j, r, head] = jnp.concatenate(rows, axis=0).astype(qkv_ref.dtype)
+
     values = tok_ref[...].astype(jnp.float32)
     full[0, hid] = layer_norm(values, gain_ref[...]).astype(full.dtype)
     greeted()
@@ -114,8 +136,13 @@
                 sent.append(copy)
                 arriving[c].append(copy)
                 held[c].append(there)
+            if stage > 0 and pieces:
+                project_one()
         if stage == 0:
-            group_ref[...] = full[0]
+            while len(pieces) > CHUNKS * (len(orders[0]) - 1):
+                project_one()
+    while pieces:
+        project_one()
     w_copy.wait()
     rows = half * full.shape[1] * full.shape[2]
     for side in range(2):
@@ -135,9 +162,11 @@
 
 
 def reduce_kernel(
-    req_count, hid_count, hidden_ref, proj_ref, w_hbm, out_ref,
-    w_ref, part, landed, total, leaving, hid_landed,
-    w_sem, req_send, req_recv, hid_send, hid_recv,
+    req_count, hid_count, lengths_ref, bounds_ref, hidden_ref, qkv_ref,
+    w_hbm, keys_hbm, values_hbm, tail_keys_hbm, tail_values_hbm, out_hbm, out_ref,
+    w_ref, keys, values, tail_keys, tail_values, out_w, attended,
+    part, landed, total, leaving, hid_landed,
+    w_sem, cache_sem, out_sem, req_send, req_recv, hid_send, hid_recv,
 ):
     req, hid = lax.axis_index("req"), lax.axis_index("hid")
     orders = reduce_orders(req_count)
@@ -152,6 +181,59 @@
         )
         copy.start()
         w_copies.append(copy)
+    _, requests, heads, request_rows, _ = qkv_ref.shape
+    own = request_rows // hid_count
+    cache_copies = []
+    for r in range(requests):
+        pairs = (
+            (keys_hbm, keys), (tail_keys_hbm, tail_keys), (values_hbm, values), (tail_values_hbm, tail_values),
+        )
+        for i, (source, target) in enumerate(pairs):
+            copy = pltpu.make_async_copy(source.at[r], target.at[r], cache_sem.at[r, i])
+            copy.start()
+            cache_copies.append(copy)
+    out_copy = pltpu.make_async_copy(out_hbm, out_w, out_sem)
+    out_copy.start()
+    units = [(r, head) for r in range(requests) for head in range(heads)]
+
+    def scores_of(query, some_keys):
+        return lax.dot_general(
+            query, some_keys, (((1,), (1,)), ((), ())), preferred_element_type=jnp.float32
+        ) * HEAD_DIM ** (-0.5)
+
+    def attend_one():
+        r, head = units.pop(0)
+        if head == 0:
+            for copy in cache_copies[4 * r : 4 * r + 4]:
+                copy.wait()
+        at = slice(head * HEAD_DIM, (head + 1) * HEAD_DIM)
+        query = qkv_ref[0, r, head]
+        prompt = scores_of(query, keys[r, :, at])
+        tail = scores_of(query, tail_keys[r, :, at])
+        fresh = scores_of(query, qkv_ref[1, r, head])
+        bounds = bounds_ref[r]
+        spot = lax.broadcasted_iota(jnp.int32, prompt.shape, 1)
+        prompt = jnp.where(spot < lengths_ref[r], prompt, very_low)
+        spot = lax.broadcasted_iota(jnp.int32, tail.shape, 1)
+        tail = jnp.where((spot >= bounds[:, 0:1]) & (spot < bounds[:, 1:2]), tail, very_low)
+        spot = lax.broadcasted_iota(jnp.int32, fresh.shape, 1)
+        fresh = jnp.where((spot >= bounds[:, 2:3]) & (spot <= bounds[:, 3:4]), fresh, very_low)
+        highest = functools.reduce(
+            jnp.maximum, [jnp.max(some, axis=1, keepdims=True) for some in (prompt, tail, fresh)]
+        )
+        totals, accrued = 0.0, 0.0
+        for some, some_values in (
+            (prompt, values[r, :, at]), (tail, tail_values[r, :, at]), (fresh, qkv_ref[2, r, head]),
+        ):
+            weights = jnp.exp(some - highest)
+            totals = totals + jnp.sum(weights, axis=1, keepdims=True)
+            accrued = accrued + jnp.dot(
+                weights.astype(jnp.bfloat16), some_values, preferred_element_type=jnp.float32
+            )
+        attended[r * request_rows : (r + 1) * request_rows, at] = (accrued / totals).astype(
+            attended.dtype
+        )
+
     sent = []
 
     def send(c, slot, bit):
@@ -191,12 +273,25 @@
                 if slot & bit:
                     arriving[c][slot] = send(c, slot, bit)
             active[c] = [slot for slot in active[c] if not slot & bit]
+            if units:
+                attend_one()
+    while units:
+        attend_one()
+    out_copy.wait()
     hid_copies = []
     for c in range(CHUNKS):
         last = orders[c][-1]
+        projected = jnp.dot(
+            attended[...], out_w[:, c * width : (c + 1) * width], preferred_element_type=jnp.float32
+        )
+        spans = [
+            projected[r * request_rows + h * own : r * request_rows + (h + 1) * own]
+            for h in range(hid_count)
+            for r in range(requests)
+        ]
         arriving[c][last].wait_recv()
         both = part[c, 0].astype(jnp.float32) + landed[c, last - 1].astype(jnp.float32)
-        both = both + proj_ref[:, :, c * width : (c + 1) * width]
+        both = both + jnp.concatenate(spans, axis=0).reshape(both.shape)
         total[c] = both
         leaving[c] = both.astype(leaving.dtype)
         for step in range(1, hid_count):
@@ -225,58 +320,69 @@
 
 def params(collective_id):
     return pltpu.CompilerParams(
-        collective_id=collective_id, has_side_effects=True, vmem_limit_bytes=48 * 2**20
-    )
-
-
-def gather_up(own_tokens, gain, in_weight):
+        collective_id=collective_id, has_side_effects=True, vmem_limit_bytes=58 * 2**20
+    )
+
+
+def gather_up(own_tokens, gain, table, in_weight, qkv_weight, requests):
     req_count, hid_count = lax.axis_size("req"), lax.axis_size("hid")
     rows, width = own_tokens.shape
     units = in_weight.shape[1]
+    slab = qkv_weight.shape[2]
     side_rows = req_count // 2 * hid_count * rows
     dma = pltpu.SemaphoreType.DMA
     return pl.pallas_call(
         functools.partial(gather_kernel, req_count, hid_count),
         out_shape=(
-            jax.ShapeDtypeStruct((hid_count, rows, width), jnp.bfloat16),
+            jax.ShapeDtypeStruct(
+                (3, requests, slab // HEAD_DIM, hid_count * rows // requests, HEAD_DIM), jnp.bfloat16
+            ),
             jax.ShapeDtypeStruct((2, side_rows, units), jnp.bfloat16),
         ),
-        in_specs=in_vmem(2) + [pl.BlockSpec(memory_space=pl.ANY)],
+        in_specs=in_vmem(3) + [pl.BlockSpec(memory_space=pl.ANY)] * 2,
         out_specs=tuple(in_vmem(2)),
         scratch_shapes=[
             pltpu.VMEM((req_count, hid_count, rows, width), jnp.bfloat16),
             pltpu.VMEM((width, units), jnp.bfloat16),
+            pltpu.VMEM(qkv_weight.shape, jnp.bfloat16),
             pltpu.VMEM((side_rows, units), jnp.float32),
             dma((CHUNKS, hid_count - 1)),
             dma((CHUNKS, hid_count - 1)),
             dma((CHUNKS, req_count - 1)),
             dma((CHUNKS, req_count - 1)),
             dma(()),
+            dma((3,)),
         ],
         compiler_params=params(0),
         name="gather_up",
-    )(own_tokens, gain.reshape(1, width), in_weight)
-
-
-def down_reduce(hidden_units, projected, down_weight):
+    )(own_tokens, gain.reshape(1, width), table, in_weight, qkv_weight)
+
+
+def down_reduce(rows, lengths, bounds, hidden_units, qkv, down_weight, caches, out_weight):
     req_count, hid_count = lax.axis_size("req"), lax.axis_size("hid")
-    _, rows, width = projected.shape
-    units = down_weight.shape[0]
+    units, width = down_weight.shape
     part_width = width // CHUNKS
     dma = pltpu.SemaphoreType.DMA
     return pl.pallas_call(
         functools.partial(reduce_kernel, req_count, hid_count),
         out_shape=jax.ShapeDtypeStruct((rows, width), jnp.float32),
-        in_specs=in_vmem(2) + [pl.BlockSpec(memory_space=pl.ANY)],
+        in_specs=[pl.BlockSpec(memory_space=pltpu.SMEM)]
+        + in_vmem(3)
+        + [pl.BlockSpec(memory_space=pl.ANY)] * 6,
         out_specs=in_vmem(1)[0],
         scratch_shapes=[
             pltpu.VMEM((CHUNKS, units, part_width), jnp.bfloat16),
+            *(pltpu.VMEM(cache.shape, jnp.bfloat16) for cache in caches),
+            pltpu.VMEM(out_weight.shape, jnp.bfloat16),
+            pltpu.VMEM((hid_count * rows, out_weight.shape[0]), jnp.bfloat16),
             pltpu.VMEM((CHUNKS, req_count, hid_count, rows, part_width), jnp.bfloat16),
             pltpu.VMEM((CHUNKS, req_count - 1, hid_count, rows, part_width), jnp.bfloat16),
             pltpu.VMEM((CHUNKS, hid_count, rows, part_width), jnp.float32),
             pltpu.VMEM((CHUNKS, hid_count, rows, part_width), jnp.bfloat16),
             pltpu.VMEM((CHUNKS, hid_count - 1, rows, part_width), jnp.bfloat16),
             dma((CHUNKS,)),
+            dma((lengths.shape[0], 4)),
+            dma(()),
             dma((CHUNKS, req_count - 1)),
             dma((CHUNKS, req_count - 1)),
             dma((CHUNKS, hid_count - 1)),
@@ -284,7 +390,7 @@
         ],
         compiler_params=params(1),
         name="down_reduce",
-    )(hidden_units, projected, down_weight)
+    )(lengths, bounds, hidden_units, qkv, down_weight, *caches, out_weight)
 
 
 def shards(
@@ -307,101 +413,41 @@
     own_rows = req_dev * samp_dev * fresh
     own_tokens = tokens.reshape(own_rows, width)
     residual = own_tokens.astype(jnp.float32)
-    group_normed, hidden_units = gather_up(own_tokens, input_gain, in_weight)
-    slab_rows, triple, slab_cols = qkv_weight.shape
     hid_count = lax.axis_size("hid")
-    group_rows = own_rows * hid_count
-    mixed_qkv = jnp.einsum(
-        "nd,jdc->jnc",
-        group_normed.reshape(group_rows, width),
-        jnp.transpose(qkv_weight, (1, 0, 2)),
-        preferred_element_type=jnp.float32,
-    ).astype(jnp.bfloat16)
-    mixed_qkv = jnp.transpose(mixed_qkv, (1, 0, 2))
-    heads_here = slab_cols // HEAD_DIM
     samples = hid_count * samp_dev
-    grouped = mixed_qkv.reshape(hid_count, req_dev, samp_dev, fresh, triple, heads_here, HEAD_DIM)
-    grouped = jnp.transpose(grouped, (1, 0, 2, 3, 4, 5, 6)).reshape(
-        req_dev, samples, fresh, triple, heads_here, HEAD_DIM
-    )
     positions = (
         prompt_lengths[:, None, None]
         + tail_lengths[:, :, None]
         + jnp.arange(fresh, dtype=jnp.int32)[None, None, :]
     )
-    queries = rotate(grouped[:, :, :, 0].astype(jnp.float32), positions).astype(jnp.bfloat16)
-    new_keys = rotate(grouped[:, :, :, 1].astype(jnp.float32), positions).astype(jnp.bfloat16)
-    new_values = grouped[:, :, :, 2]
-    prompt_len = prompt_keys.shape[1]
-    cached_keys = prompt_keys.reshape(req_dev, prompt_len, heads_here, HEAD_DIM)
-    cached_values = prompt_values.reshape(req_dev, prompt_len, heads_here, HEAD_DIM)
-    prompt_queries = queries.reshape(req_dev, samples * fresh, heads_here, HEAD_DIM)
-    score_scale = HEAD_DIM ** (-0.5)
-    prompt_scores = (
-        jnp.einsum(
-            "rqhd,rkhd->rqhk", prompt_queries, cached_keys, preferred_element_type=jnp.float32
-        )
-        * score_scale
-    )
-    keeping = (jnp.arange(prompt_len, dtype=jnp.int32)[None, :] < prompt_lengths[:, None])[
-        :, None, None, :
-    ]
-    prompt_scores = jnp.where(keeping, prompt_scores, very_low)
-    peaks = jnp.max(prompt_scores, axis=-1)
-    prompt_weights = jnp.where(keeping, jnp.exp(prompt_scores - peaks[..., None]), 0.0)
-    totals = jnp.sum(prompt_weights, axis=-1)
-    accrued = jnp.einsum(
-        "rqhk,rkhd->rqhd",
-        prompt_weights.astype(jnp.bfloat16),
-        cached_values,
-        preferred_element_type=jnp.float32,
-    )
-    peaks = peaks.reshape(req_dev, samples, fresh, heads_here)
-    totals = totals.reshape(req_dev, samples, fresh, heads_here)
-    accrued = accrued.reshape(req_dev, samples, fresh, heads_here, HEAD_DIM)
-    tail_len = tail_keys.shape[2]
-    later_keys = tail_keys.reshape(req_dev, samples, tail_len, heads_here, HEAD_DIM)
-    later_values = tail_values.reshape(req_dev, samples, tail_len, heads_here, HEAD_DIM)
-    tail_scores = (
-        jnp.einsum("rsthd,rskhd->rsthk", queries, later_keys, preferred_element_type=jnp.float32)
-        * score_scale
-    )
-    tail_keep = (jnp.arange(tail_len, dtype=jnp.int32)[None, None, :] < tail_lengths[:, :, None])[
-        :, :, None, None, :
-    ]
-    self_scores = (
-        jnp.einsum("rsthd,rsuhd->rsthu", queries, new_keys, preferred_element_type=jnp.float32)
-        * score_scale
-    )
-    position_order = jnp.arange(fresh, dtype=jnp.int32)
-    self_keep = (position_order[None, :] <= position_order[:, None])[None, None, :, None, :]
-    highest = jnp.maximum(peaks, jnp.max(jnp.where(tail_keep, tail_scores, very_low), axis=-1))
-    highest = jnp.maximum(highest, jnp.max(jnp.where(self_keep, self_scores, very_low), axis=-1))
-    scaling = jnp.exp(peaks - highest)
-    tail_weights = jnp.where(tail_keep, jnp.exp(tail_scores - highest[..., None]), 0.0)
-    self_weights = jnp.where(self_keep, jnp.exp(self_scores - highest[..., None]), 0.0)
-    totals = totals * scaling + jnp.sum(tail_weights, axis=-1) + jnp.sum(self_weights, axis=-1)
-    accrued = accrued * scaling[..., None]
-    accrued = accrued + jnp.einsum(
-        "rsthk,rskhd->rsthd",
-        tail_weights.astype(jnp.bfloat16),
-        later_values,
-        preferred_element_type=jnp.float32,
-    )
-    accrued = accrued + jnp.einsum(
-        "rsthu,rsuhd->rsthd",
-        self_weights.astype(jnp.bfloat16),
-        new_values,
-        preferred_element_type=jnp.float32,
-    )
-    attended = (accrued / totals[..., None]).astype(jnp.bfloat16)
-    attended = attended.reshape(req_dev, hid_count, samp_dev, fresh, heads_here * HEAD_DIM)
-    attended_rows = jnp.transpose(attended, (1, 0, 2, 3, 4)).reshape(
-        group_rows, heads_here * HEAD_DIM
-    )
-    projected = jnp.dot(attended_rows, out_weight, preferred_element_type=jnp.float32)
+    row_positions = jnp.transpose(
+        positions.reshape(req_dev, hid_count, samp_dev, fresh), (1, 0, 2, 3)
+    ).reshape(hid_count * own_rows)
+    qkv, hidden_units = gather_up(
+        own_tokens, input_gain, rotation_table(row_positions), in_weight,
+        jnp.transpose(qkv_weight, (1, 0, 2)), req_dev,
+    )
+    tail_len, slab = tail_keys.shape[2:]
+    row = jnp.arange(samples * fresh, dtype=jnp.int32)
+    sample = row // fresh
+    first_tail = jnp.broadcast_to(sample * tail_len, (req_dev, samples * fresh))
+    bounds = jnp.stack(
+        [
+            first_tail,
+            first_tail + jnp.repeat(tail_lengths, fresh, axis=1),
+            jnp.broadcast_to(sample * fresh, first_tail.shape),
+            jnp.broadcast_to(row, first_tail.shape),
+        ],
+        axis=-1,
+    )
+    caches = (
+        prompt_keys,
+        prompt_values,
+        tail_keys.reshape(req_dev, samples * tail_len, slab),
+        tail_values.reshape(req_dev, samples * tail_len, slab),
+    )
     branch_sum = down_reduce(
-        hidden_units, projected.reshape(hid_count, own_rows, width), down_weight
+        own_rows, prompt_lengths, bounds, hidden_units, qkv, down_weight, caches, out_weight
     )
     final_state = residual + branch_sum
     next_hidden = final_state.astype(jnp.bfloat16).reshape(req_dev, samp_dev, fresh, width)

time: 127 us -> 91.1 us (0.72)
  matrix products: 33.8 us -> 0 us
  local copies, waits for them, and re-layouts: 11.8 us -> 3.65 us
  Pallas kernels: 72.4 us -> 80.5 us
  other arithmetic: 8.06 us -> 5.91 us
    dot_general x8 -> x0, matrix products: 33.8 us -> none  [the longest x1 10.5 us: shards(): jnp.einsum('nd,jdc->jnc', group_normed.reshape(group_rows, width), jnp.tr...]
    pallas_call x1, Pallas kernels: 36.1 us -> 40.9 us  [down_reduce(): pl.pallas_call(functools.partial(reduce_kernel, req_count, hid_count), ou...]
    pallas_call x1, Pallas kernels: 36.3 us -> 39.6 us  [gather_up(): pl.pallas_call(functools.partial(gather_kernel, req_count, hid_count), ou...]
    unnamed x9, local copies, waits for them, and re-layouts: 3.59 us -> 0.69 us
    another operation x2 -> x3, local copies, waits for them, and re-layouts: 2.78 us -> 0.15 us  [shards(): jnp.stack([first_tail, first_tail + jnp.repeat(tail_lengths, fresh, axis=...]
    lt x2 -> x0, other arithmetic: 1.49 us -> none  [the longest x1 0.75 us: shards(): jnp.arange(tail_len, dtype=jnp.int32)[None, None, :]]
    reshape x9 -> x1, local copies, waits for them, and re-layouts: 1.37 us -> 0.07 us  [shards(): jnp.repeat(tail_lengths, fresh, axis=1)]
where the time goes in v2:
time: 91.1 us; the launch traced here: 90.8 us
  Pallas kernels  80.5 us (88%)
  other arithmetic  5.91 us (6%)
  local copies, waits for them, and re-layouts  3.65 us (4%)
    pallas_call x1, Pallas kernels, down_reduce(): pl.pallas_call(functools.partial(reduce_kernel, req_count, hid_count), ou...  40.9 us
    pallas_call x1, Pallas kernels, gather_up(): pl.pallas_call(functools.partial(gather_kernel, req_count, hid_count), ou...  39.6 us

profile of v2, /device:TPU:0, one launch (start us, length us, event | category | flops | bytes accessed | tf_op | source)
XLA Modules:
  0.0 90.8 jit_solution(13247568270171838393)
XLA Ops:
  0.6 0.8 broadcast_add_fusion.1
  1.4 0.1 add.72
  1.5 0.1 add_convert_fusion
  1.6 0.1 convert_element_type.28
  1.7 0.2 multiply_cosine_fusion
  1.9 0.6 pad_maximum_fusion.table_ref
  2.5 1.6 %reshape.229.tok_ref = bf16[16,4096]{1,0:T(8,128)(2,1)} reshape(bf16[2,4,2,4096]{3,2,1,0:T(2,128)(2,1)} %param.14) | data formatting | bytes 262144 | tf_op jit(solution)/shard_map/reshape | solution.py:414
  4.1 0.0 copy-start.3
  4.1 39.6 %gather_up.1 = (bf16[3,2,4,32,256]{4,3,2,1,0:T(8,128)(2,1)}, bf16[2,256,512]{2,1,0:T(8,128)(2,1)}) custom-call(bf16[16,4096]{1,0:T(8,128)(2,1)} %reshape.229.tok_ref, f32[1,4096]{1,0:T(1,128)} %bitcast.8, f32[2,64,128]{2,1,0:T(8,128)} %pad_maximum_fusion.table_ref, bf16[4096,512]{1,0:T(8,128)(2,1)} %w_hbm.2, bf16[3,4096,1024]{2,1,0:T(8,128)(2,1)} %bitcast.5), custom_call_target="tpu_custom_call" | custom-call | tf_op jit(solution)/shard_map/gather_up/pallas_call | solution.py:334
  43.7 0.0 copy-done.3
  43.8 0.1 broadcast_in_dim.14
  43.8 0.1 reshape.236
  43.9 0.1 broadcast_add_fusion
  44.0 0.1 stack_broadcast_in_dim.11.clone
  44.1 0.1 stack_broadcast_in_dim.12
  44.1 0.7 pad_add_fusion.bounds_ref
  44.8 0.0 copy-start
  44.8 0.0 copy-start.2
  44.8 0.0 copy-start.1
  44.8 40.9 %down_reduce.1 = f32[16,4096]{1,0:T(8,128)} custom-call(s32[2]{0:T(128)} %lengths_ref.1, s32[2,32,4]{2,1,0:T(8,128)} %pad_add_fusion.bounds_ref, bf16[2,256,512]{2,1,0:T(8,128)(2,1)} %get-tuple-element.4.hidden_ref, bf16[3,2,4,32,256]{4,3,2,1,0:T(8,128)(2,1)} %get-tuple-element.5.qkv_ref, bf16[512,4096]{1,0:T(8,128)(2,1)} %w_hbm.3, ...), custom_call_target="tpu_custom_call" | custom-call | tf_op jit(solution)/shard_map/down_reduce/pallas_call | solution.py:366
  85.8 0.0 copy-done
  85.8 1.1 %fusion.1 = f32[16]{0:T(128)S(1)} fusion(f32[16,4096]{1,0:T(8,128)} %down_reduce.1, bf16[16,4096]{1,0:T(8,128)(2,1)S(1)} %copy-done), kind=kLoop, calls=%fused_computation.8 | loop fusion | flops 196592 | bytes 393280 | tf_op jit(solution)/shard_map/reduce_sum | solution.py:18
  86.9 1.2 %multiply_reduce_fusion.1 = f32[16]{0:T(128)S(1)} fusion(f32[16]{0:T(128)S(1)} %broadcast_multiply_fusion, f32[16,4096]{1,0:T(8,128)} %down_reduce.1, bf16[16,4096]{1,0:T(8,128)(2,1)S(1)} %copy-done), kind=kLoop, calls=%fused_computation.1 | loop fusion | flops 327664 | bytes 393344 | tf_op jit(solution)/shard_map/reduce_sum | solution.py:20
  88.1 0.0 copy-done.2
  88.1 0.0 copy-done.1
  88.1 1.2 %multiply_reduce_fusion = (f32[16]{0:T(128)S(1)}, bf16[16,4096]{1,0:T(8,128)(2,1)S(1)}) fusion(f32[4096]{0:T(1024)S(1)} %convert_element_type.31, f32[4096]{0:T(1024)S(1)} %copy-done.1, f32[16]{0:T(128)S(1)} %add_rsqrt_fusion, f32[16]{0:T(128)S(1)} %broadcast_multiply_fusion, f32[16,4096]{1,0:T(8,128)} %down_reduce.1, bf16[16,4096]{1,0:T(8,128)(2,1)S(1)} %copy-done), kind=kLoop, calls=%fused_computation | loop fusion | flops 524272 | bytes 557248 | tf_op jit(solution)/shard_map/reduce_sum | solution.py:454
  89.3 0.8 reshape.234
  90.0 0.1 reshape.235
  90.1 0.7 copy.34
  (8 shorter events, 0.0 us)
Async XLA Ops:
  4.1 39.6 %copy-start.3 = (s32[2,16]{1,0:T(2,128)S(1)}, s32[2,16]{1,0:T(2,128)}, u32[]{:S(2)}) copy-start(s32[2,16]{1,0:T(2,128)} %param.27) | copy-start | bytes 388
  44.8 41.0 %copy-start = (bf16[16,4096]{1,0:T(8,128)(2,1)S(1)}, bf16[16,4096]{1,0:T(8,128)(2,1)}, u32[]{:S(2)}) copy-start(bf16[16,4096]{1,0:T(8,128)(2,1)} %reshape.229.tok_ref) | copy-start | bytes 393220
  44.8 43.2 %copy-start.2 = (bf16[4096]{0:T(1024)(128)(2,1)S(1)}, bf16[4096]{0:T(1024)(128)(2,1)}, u32[]{:S(2)}) copy-start(bf16[4096]{0:T(1024)(128)(2,1)} %param.21) | copy-start | bytes 24580
  44.8 43.3 %copy-start.1 = (f32[4096]{0:T(1024)S(1)}, f32[4096]{0:T(1024)}, u32[]{:S(2)}) copy-start(f32[4096]{0:T(1024)} %param.20) | copy-start | bytes 49156

commit v3 on v2

--- a/solution.py
+++ b/solution.py
@@ -67,7 +67,7 @@
 
 def gather_kernel(
     req_count, hid_count, tok_ref, gain_ref, table_ref, w_hbm, qkv_hbm, qkv_ref, hidden_ref,
-    full, w_ref, qkv_w, total, hid_send, hid_recv, req_send, req_recv, w_sem, qkv_sem,
+    full, w_ref, qkv_w, qkv_total, total, hid_send, hid_recv, req_send, req_recv, w_sem, qkv_sem,
 ):
     req, hid = lax.axis_index("req"), lax.axis_index("hid")
     orders = [order[::-1] for order in reduce_orders(req_count)]
@@ -83,22 +83,33 @@
     w_copy.start()
     _, requests, heads, request_rows, _ = qkv_ref.shape
     own = request_rows // hid_count
-    pieces = [(j, head) for j in range(3) for head in range(heads)]
+    pieces = [(c, j) for c in range(CHUNKS) for j in range(3)]
+    piece_count = len(pieces)
 
     def project_one():
-        j, head = pieces.pop(0)
-        if head == 0:
+        c, j = pieces.pop(0)
+        if c == 0:
             qkv_copies[j].wait()
-        group = full[0].reshape(hid_count * full.shape[2], full.shape[3])
+        group = full[0, :, :, c * width : (c + 1) * width].reshape(hid_count * full.shape[2], width)
         value = jnp.dot(
-            group, qkv_w[j, :, head * HEAD_DIM : (head + 1) * HEAD_DIM],
-            preferred_element_type=jnp.float32,
-        ).astype(jnp.bfloat16).astype(jnp.float32)
-        if j < 2:
-            value = turn(value, table_ref[...])
-        for r in range(requests):
-            rows = [value[(h * requests + r) * own : (h * requests + r + 1) * own] for h in range(hid_count)]
-            qkv_ref[j, r, head] = jnp.concatenate(rows, axis=0).astype(qkv_ref.dtype)
+            group, qkv_w[j, c * width : (c + 1) * width, :], preferred_element_type=jnp.float32
+        )
+        if c > 0:
+            value = value + qkv_total[j]
+        if c < CHUNKS - 1:
+            qkv_total[j] = value
+            return
+        value = value.astype(jnp.bfloat16).astype(jnp.float32)
+        for head in range(heads):
+            part = value[:, head * HEAD_DIM : (head + 1) * HEAD_DIM]
+            if j < 2:
+                part = turn(part, table_ref[...])
+            for r in range(requests):
+                rows = [
+                    part[(h * requests + r) * own : (h * requests + r + 1) * own]
+                    for h in range(hid_count)
+                ]
+                qkv_ref[j, r, head] = jnp.concatenate(rows, axis=0).astype(qkv_ref.dtype)
 
     values = tok_ref[...].astype(jnp.float32)
     full[0, hid] = layer_norm(values, gain_ref[...]).astype(full.dtype)
@@ -136,10 +147,10 @@
                 sent.append(copy)
                 arriving[c].append(copy)
                 held[c].append(there)
-            if stage > 0 and pieces:
-                project_one()
-        if stage == 0:
-            while len(pieces) > CHUNKS * (len(orders[0]) - 1):
+            if stage == 0:
+                while len(pieces) > piece_count - 2 * (c + 1):
+                    project_one()
+            elif pieces:
                 project_one()
     while pieces:
         project_one()
@@ -162,8 +173,9 @@
 
 
 def reduce_kernel(
-    req_count, hid_count, lengths_ref, bounds_ref, hidden_ref, qkv_ref,
-    w_hbm, keys_hbm, values_hbm, tail_keys_hbm, tail_values_hbm, out_hbm, out_ref,
+    req_count, hid_count, lengths_ref, bounds_ref, tok_ref, gain_ref, score_w_ref, hidden_ref, qkv_ref,
+    w_hbm, keys_hbm, values_hbm, tail_keys_hbm, tail_values_hbm, out_hbm, next_ref, score_ref,
+    state,
     w_ref, keys, values, tail_keys, tail_values, out_w, attended,
     part, landed, total, leaving, hid_landed,
     w_sem, cache_sem, out_sem, req_send, req_recv, hid_send, hid_recv,
@@ -309,7 +321,12 @@
         for step in range(1, hid_count):
             hid_copies[c * (hid_count - 1) + step - 1].wait_recv()
             value = value + hid_landed[c, step - 1].astype(jnp.float32)
-        out_ref[:, c * width : (c + 1) * width] = value
+        at = slice(c * width, (c + 1) * width)
+        value = value + tok_ref[:, at].astype(jnp.float32)
+        state[:, at] = value
+        next_ref[:, at] = value.astype(next_ref.dtype)
+    scored = layer_norm(state[...], gain_ref[...]) * score_w_ref[...].astype(jnp.float32)
+    score_ref[...] = jnp.broadcast_to(jnp.sum(scored, axis=-1, keepdims=True), score_ref.shape)
     for copy in sent:
         copy.wait_send()
 
@@ -345,6 +362,7 @@
             pltpu.VMEM((req_count, hid_count, rows, width), jnp.bfloat16),
             pltpu.VMEM((width, units), jnp.bfloat16),
             pltpu.VMEM(qkv_weight.shape, jnp.bfloat16),
+            pltpu.VMEM((3, hid_count * rows, slab), jnp.float32),
             pltpu.VMEM((side_rows, units), jnp.float32),
             dma((CHUNKS, hid_count - 1)),
             dma((CHUNKS, hid_count - 1)),
@@ -358,19 +376,24 @@
     )(own_tokens, gain.reshape(1, width), table, in_weight, qkv_weight)
 
 
-def down_reduce(rows, lengths, bounds, hidden_units, qkv, down_weight, caches, out_weight):
+def down_reduce(own_tokens, gain, score_weight, lengths, bounds, hidden_units, qkv, down_weight, caches, out_weight):
     req_count, hid_count = lax.axis_size("req"), lax.axis_size("hid")
     units, width = down_weight.shape
+    rows = own_tokens.shape[0]
     part_width = width // CHUNKS
     dma = pltpu.SemaphoreType.DMA
     return pl.pallas_call(
         functools.partial(reduce_kernel, req_count, hid_count),
-        out_shape=jax.ShapeDtypeStruct((rows, width), jnp.float32),
+        out_shape=(
+            jax.ShapeDtypeStruct((rows, width), jnp.bfloat16),
+            jax.ShapeDtypeStruct((rows, 128), jnp.float32),
+        ),
         in_specs=[pl.BlockSpec(memory_space=pltpu.SMEM)]
-        + in_vmem(3)
+        + in_vmem(6)
         + [pl.BlockSpec(memory_space=pl.ANY)] * 6,
-        out_specs=in_vmem(1)[0],
+        out_specs=tuple(in_vmem(2)),
         scratch_shapes=[
+            pltpu.VMEM((rows, width), jnp.float32),
             pltpu.VMEM((CHUNKS, units, part_width), jnp.bfloat16),
             *(pltpu.VMEM(cache.shape, jnp.bfloat16) for cache in caches),
             pltpu.VMEM(out_weight.shape, jnp.bfloat16),
@@ -390,7 +413,10 @@
         ],
         compiler_params=params(1),
         name="down_reduce",
-    )(lengths, bounds, hidden_units, qkv, down_weight, *caches, out_weight)
+    )(
+        lengths, bounds, own_tokens, gain.reshape(1, width), score_weight.reshape(1, width),
+        hidden_units, qkv, down_weight, *caches, out_weight,
+    )
 
 
 def shards(
@@ -412,7 +438,6 @@
     req_dev, samp_dev, fresh, width = tokens.shape
     own_rows = req_dev * samp_dev * fresh
     own_tokens = tokens.reshape(own_rows, width)
-    residual = own_tokens.astype(jnp.float32)
     hid_count = lax.axis_size("hid")
     samples = hid_count * samp_dev
     positions = (
@@ -446,14 +471,12 @@
         tail_keys.reshape(req_dev, samples * tail_len, slab),
         tail_values.reshape(req_dev, samples * tail_len, slab),
     )
-    branch_sum = down_reduce(
-        own_rows, prompt_lengths, bounds, hidden_units, qkv, down_weight, caches, out_weight
-    )
-    final_state = residual + branch_sum
-    next_hidden = final_state.astype(jnp.bfloat16).reshape(req_dev, samp_dev, fresh, width)
-    sample_scores = jnp.sum(
-        layer_norm(final_state, final_gain) * score_weight.astype(jnp.float32), axis=-1
-    )
+    next_hidden, sample_scores = down_reduce(
+        own_tokens, final_gain, score_weight, prompt_lengths, bounds, hidden_units, qkv,
+        down_weight, caches, out_weight,
+    )
+    next_hidden = next_hidden.reshape(req_dev, samp_dev, fresh, width)
+    sample_scores = sample_scores[:, 0]
     return (next_hidden, sample_scores.reshape(req_dev, samp_dev, fresh))
 
 

time: 91.1 us -> 92 us (level)
  local copies, waits for them, and re-layouts: 3.65 us -> 7.35 us
  other arithmetic: 5.91 us -> 2.47 us
    reduce_sum x3 -> x0, other arithmetic: 3.44 us -> none  [the longest x1 1.17 us: shards(): jnp.sum(layer_norm(final_state, final_gain) * score_weight.astype(jnp.flo...]
    pallas_call x1, Pallas kernels: 40.9 us -> 43.1 us  [down_reduce(): pl.pallas_call(functools.partial(reduce_kernel, req_count, hid_count), ou...]
    reshape x2, local copies, waits for them, and re-layouts: 0.85 us -> 2.98 us  [the longest x1 1.67 us: shards(): next_hidden = next_hidden.reshape(req_dev, samp_dev, fresh, width)]
    pallas_call x1, Pallas kernels: 39.6 us -> 38.1 us  [gather_up(): pl.pallas_call(functools.partial(gather_kernel, req_count, hid_count), ou...]
where the time goes in v3:
time: 92 us; the launch traced here: 91.7 us
  Pallas kernels  81.2 us (88%)
  local copies, waits for them, and re-layouts  7.35 us (8%)
  other arithmetic  2.47 us (3%)
    pallas_call x1, Pallas kernels, down_reduce(): pl.pallas_call(functools.partial(reduce_kernel, req_count, hid_count), ou...  43.1 us
    pallas_call x1, Pallas kernels, gather_up(): pl.pallas_call(functools.partial(gather_kernel, req_count, hid_count), ou...  38.1 us

profile of v3, /device:TPU:0, one launch (start us, length us, event | category | flops | bytes accessed | tf_op | source)
XLA Modules:
  0.0 91.7 jit_solution(15759401107199217609)
XLA Ops:
  0.7 0.8 broadcast_add_fusion.1
  1.4 0.1 add.61
  1.5 0.1 add_convert_fusion
  1.6 0.1 convert_element_type.18
  1.7 1.3 %reshape.221.score_w_ref = bf16[1,4096]{1,0:T(2,128)(2,1)} reshape(bf16[4096]{0:T(1024)(128)(2,1)} %param.21) | data formatting | bytes 16384 | tf_op jit(solution)/shard_map/reshape | solution.py:417
  3.0 0.7 broadcast_in_dim.22
  3.8 0.1 reshape.226
  3.8 0.1 broadcast_add_fusion
  3.9 0.1 stack_broadcast_in_dim.11.clone
  4.0 0.1 stack_broadcast_in_dim.12
  4.1 0.7 pad_add_fusion.bounds_ref
  4.8 0.2 multiply_cosine_fusion
  5.0 0.6 pad_maximum_fusion.table_ref
  5.6 1.6 %reshape.219.tok_ref = bf16[16,4096]{1,0:T(8,128)(2,1)} reshape(bf16[2,4,2,4096]{3,2,1,0:T(2,128)(2,1)} %param.14) | data formatting | bytes 262144 | tf_op jit(solution)/shard_map/reshape | solution.py:440
  7.2 38.1 %gather_up.1 = (bf16[3,2,4,32,256]{4,3,2,1,0:T(8,128)(2,1)}, bf16[2,256,512]{2,1,0:T(8,128)(2,1)}) custom-call(bf16[16,4096]{1,0:T(8,128)(2,1)} %reshape.219.tok_ref, f32[1,4096]{1,0:T(1,128)} %bitcast.10, f32[2,64,128]{2,1,0:T(8,128)} %pad_maximum_fusion.table_ref, bf16[4096,512]{1,0:T(8,128)(2,1)} %w_hbm.2, bf16[3,4096,1024]{2,1,0:T(8,128)(2,1)} %bitcast.6), custom_call_target="tpu_custom_call" | custom-call | tf_op jit(solution)/shard_map/gather_up/pallas_call | solution.py:351
  45.4 43.1 %down_reduce.1 = (bf16[16,4096]{1,0:T(8,128)(2,1)}, f32[16,128]{1,0:T(8,128)}) custom-call(s32[2]{0:T(128)} %lengths_ref.1, s32[2,32,4]{2,1,0:T(8,128)} %pad_add_fusion.bounds_ref, bf16[16,4096]{1,0:T(8,128)(2,1)} %reshape.219.tok_ref, f32[1,4096]{1,0:T(1,128)} %bitcast.9, bf16[1,4096]{1,0:T(2,128)(2,1)} %reshape.221.score_w_ref, ...), custom_call_target="tpu_custom_call" | custom-call | tf_op jit(solution)/shard_map/down_reduce/pallas_call | solution.py:385
  88.5 1.7 %reshape.225 = bf16[2,4,2,4096]{3,2,1,0:T(2,128)(2,1)} reshape(bf16[16,4096]{1,0:T(8,128)(2,1)} %get-tuple-element.8) | data formatting | bytes 262144 | tf_op jit(solution)/shard_map/reshape | solution.py:478
  90.1 0.8 slice_reduce_fusion
  91.0 0.1 reshape_squeeze.3
  91.0 0.7 copy.34
  (5 shorter events, 0.0 us)
